TPU v7x, 32 devices: a whole 2x2x4 slice. The times are simulated.
32 devices in a mesh: member: 2 (over y), wave: 4 (over z), lev: 2 (over x), fld: 2 (over core).
Axes of the slice: x: 2, y: 2, z: 4, core: 2. Of those that a mesh axis runs over, the one named last changes fastest.
Arguments:
- spectral: bfloat16 [2048, 2, 48, 1024], P(('member', 'wave'), None, ('lev', 'fld')), parts along dimension 0, may hold values from -0.1796875 to 0.1796875
- legendre: bfloat16 [1024, 64, 1024], P('wave'), may hold values from -0.1875 to 0.1875
- wave_order: int32 [1024], replicated, may hold values from 0 to 1023, as said below
Outputs:
- grid: bfloat16 [2, 24, 256, 4096], P(None, 'fld', ('member', 'wave'), 'lev'), parts along dimension 2
There are 2 independent parts, one for each index of `member`. A program takes and returns all parts, laid end to end along the dimension named above; an argument that names none is the same for every part. Nothing has to cross between parts.
Inputs may be any that keep to these rules, and one draw needn't show every extreme that they name: `wave_order`: a permutation; each block of 256 slots (the slots of one index of wave) holds 128 wavenumbers m below 512 together with 1023 - m for each, in some order.
All inputs are finite; a program needn't handle non-finite values.
Results may differ from a plain program's by a relative error of at most 0.0055.
Values may be sent and summed in bfloat16 or wider, within the bound.
No kernel may reach another device: no remote copies, remote signals or barrier semaphores. Data moves between devices by JAX's collectives and lax.ppermute only.
A program may use at most 192 MiB of HBM per device.

v0:
```python
import math

import jax
import jax.numpy as jnp
from jax import lax
from jax.sharding import PartitionSpec as P

NLON = 4096


def longitude_sum(fourier, wave_order, lon_start, width):
    slots = fourier.shape[0]
    columns_here = fourier.shape[2]
    rows_here = fourier.shape[3]
    lon_index = lon_start + jnp.arange(width, dtype=jnp.int32)
    phases = wave_order[:, None] * lon_index[None, :] % NLON
    angles = phases.astype(jnp.float32) * (2.0 * math.pi / NLON)
    weights = jnp.where(wave_order == 0, 1.0, 2.0).astype(jnp.float32)[:, None]
    cosines = (weights * jnp.cos(angles)).astype(jnp.bfloat16)
    sines = (weights * jnp.sin(angles)).astype(jnp.bfloat16)
    table = jnp.concatenate([cosines, -sines], axis=0)
    left_side = fourier.transpose(2, 3, 1, 0).reshape(columns_here * rows_here, 2 * slots)
    values = jnp.dot(left_side, table, preferred_element_type=jnp.float32)
    return values.astype(jnp.bfloat16).reshape(columns_here, rows_here, width)


def shards(spectral, legendre, wave_order):
    slots_here = spectral.shape[0]
    columns_here = spectral.shape[2]
    degree_count = legendre.shape[2]
    slot_start = lax.axis_index("wave") * slots_here
    wave_mine = lax.dynamic_slice_in_dim(wave_order, slot_start, slots_here, 0)
    degree_index = jnp.arange(degree_count, dtype=jnp.int32)
    keep = degree_index[None, :] >= wave_mine[:, None]
    coeffs = jnp.where(keep[:, None, None, :], spectral, jnp.zeros((), spectral.dtype))
    signs = (1 - 2 * ((degree_index[None, :] + wave_mine[:, None]) % 2)).astype(jnp.bfloat16)
    mirrored = jnp.concatenate([legendre, legendre * signs[:, None, :]], axis=1)
    accumulated = jnp.einsum("shn,srcn->srch", mirrored, coeffs, preferred_element_type=jnp.float32)
    fourier = accumulated.astype(jnp.bfloat16)
    lev_count = lax.axis_size("lev")
    received = lax.all_to_all(fourier, "wave", split_axis=3, concat_axis=0, tiled=True)
    width = min(512, NLON)
    pieces = [
        longitude_sum(received, wave_order, jnp.int32(start), width)
        for start in range(0, NLON, width)
    ]
    row_values = jnp.concatenate(pieces, axis=2)
    boxes = lax.all_to_all(row_values, "lev", split_axis=2, concat_axis=0, tiled=True)
    return boxes.reshape(lev_count, columns_here, boxes.shape[1], boxes.shape[2])


def solution(mesh):
    in_specs = (P(("member", "wave"), None, ("lev", "fld"), None), P("wave", None, None), P())
    out_specs = P(None, "fld", ("member", "wave"), "lev")
    return jax.shard_map(shards, mesh=mesh, in_specs=in_specs, out_specs=out_specs, check_vma=False)
```

profile of v0, /device:TPU:0, one launch (start us, length us, event | category | flops | bytes accessed | tf_op | source)
XLA Modules:
  0.0 358.3 jit_solution(2215958533714888704)
XLA Ops:
  0.0 0.8 dynamic_slice.3
  0.8 0.6 fusion.91
  1.4 0.2 iota_compare_fusion
  1.6 22.9 %broadcast_multiply_fusion = bf16[256,64,1024]{2,1,0:T(8,128)(2,1)} fusion(bf16[256,64,1024]{2,1,0:T(8,128)(2,1)} %param.4, bf16[256,1024]{1,0:T(8,128)(2,1)S(1)} %fusion.91), kind=kLoop, calls=%fused_computation.4 | loop fusion | flops 16777216 | bytes 67633152 | tf_op jit(solution)/shard_map/mul | solution.py:37
  24.5 15.3 %broadcast_select_fusion = bf16[256,2,12,1024]{3,1,2,0:T(2,128)(2,1)} fusion(bf16[256,2,12,1024]{3,1,2,0:T(2,128)(2,1)} %param.3, pred[256,1024]{1,0:T(8,128)(4,1)S(1)} %iota_compare_fusion), kind=kLoop, calls=%fused_computation.2 | loop fusion | flops 6291456 | bytes 25427968 | tf_op jit(solution)/shard_map/jit(_where)/select_n | solution.py:35
  39.9 40.0 %fusion.61 = bf16[256,2,12,128]{3,2,1,0:T(8,128)(2,1)S(1)} fusion(bf16[256,64,1024]{2,1,0:T(8,128)(2,1)} %broadcast_multiply_fusion, bf16[256,64,1024]{2,1,0:T(8,128)(2,1)} %param.4, bf16[256,2,12,1024]{3,1,2,0:T(2,128)(2,1)} %broadcast_select_fusion), kind=kOutput, calls=%fused_computation.118 | convolution fusion | flops 1745616896 | bytes 81264640 | tf_op jit(solution)/shard_map/shn,srcn->srch/dot_general | solution.py:38
  79.9 3.8 %copy.26 = bf16[256,2,12,128]{0,1,2,3:T(2,128)(2,1)} copy(bf16[256,2,12,128]{3,2,1,0:T(8,128)(2,1)S(1)} %fusion.61) | data formatting | bytes 3145728 | tf_op jit(solution)/shard_map/convert_element_type | solution.py:39
  83.7 0.0 copy-start.15
  83.8 6.7 %all-to-all-start = ((bf16[256,2,12,128]{0,1,2,3:T(2,128)(2,1)}), bf16[256,2,12,128]{0,1,2,3:T(2,128)(2,1)S(1)}, u32[]{:S(2)}, u32[]{:S(2)}) async-start(bf16[256,2,12,128]{0,1,2,3:T(2,128)(2,1)} %copy.26), calls=%async_computation | async-start | bytes 3145728 | tf_op jit(solution)/shard_map/all_to_all | solution.py:41
  90.5 0.0 copy-done.15
  90.5 63.0 %multiply_convert_fusion.1 = (bf16[1024,512]{1,0:T(8,128)(2,1)}, bf16[1024,512]{1,0:T(8,128)(2,1)}, bf16[1024,512]{1,0:T(8,128)(2,1)}, bf16[1024,512]{1,0:T(8,12...) fusion(s32[512]{0:T(512)S(1)} %get-tuple-element.21, ...), kind=kLoop, calls=%fused_computation.100 | loop fusion | flops 67108864 | bytes 8411136 | tf_op jit(solution)/shard_map/convert_element_type | solution.py:19
  153.5 64.9 %fusion.99 = (bf16[1024,512]{1,0:T(8,128)(2,1)}, bf16[1024,512]{1,0:T(8,128)(2,1)}, bf16[1024,512]{1,0:T(8,128)(2,1)}, bf16[1024,512]{1,0:T(8,128)(2,1)}, bf16[1...) fusion(s32[512]{0:T(512)S(1)} %get-tuple-element.21, ...), kind=kLoop, calls=%fused_computation.141 | loop fusion | flops 79691776 | bytes 8411136 | tf_op jit(solution)/shard_map/neg | solution.py:21
  218.4 0.0 all-to-all-done
  218.4 0.4 copy.27
  218.8 0.2 copy.35
  219.0 1.6 copy.29
  220.6 0.0 copy-start.14
  220.6 0.4 copy.36
  221.0 0.8 copy-done.14
  221.8 0.0 copy-start.11
  221.8 1.0 fusion.85
  222.9 0.2 copy-done.11
  223.0 0.3 copy-done.13
  223.4 1.0 fusion.82
  224.4 0.2 copy-done.9
  224.6 0.3 copy-done.12
  224.9 1.0 fusion.79
  225.9 0.2 copy-done.7
  226.1 0.3 copy-done.10
  226.4 1.0 fusion.76
  227.5 0.2 copy-done.5
  227.7 0.3 copy-done.8
  228.0 1.0 fusion.73
  229.0 0.2 copy-done.3
  229.2 0.3 copy-done.6
  229.5 1.0 fusion.70
  230.5 0.2 copy-done.1
  230.7 0.3 copy-done.4
  231.1 1.0 fusion.67
  232.1 0.2 copy-done
  232.3 0.3 copy-done.2
  232.6 1.0 fusion.64
  233.6 16.1 %copy.30 = bf16[12,32,4096]{1,0,2:T(8,128)(2,1)} copy(bf16[12,32,4096]{2,1,0:T(8,128)(2,1)S(1)} %constant_dynamic-update-slice_fusion) | data formatting | bytes 6291456 | tf_op jit(solution)/shard_map/concatenate | solution.py:47
  249.7 19.1 %reshape.122 = bf16[2,2,393216]{2,1,0:T(2,128)(2,1)S(1)} reshape(bf16[4096,12,32]{2,1,0:T(8,128)(2,1)} %bitcast.37) | data formatting | bytes 6291456
  268.9 39.9 %all_to_all.33 = bf16[2,2,393216]{2,1,0:T(2,128)(2,1)} all-to-all(bf16[2,2,393216]{2,1,0:T(2,128)(2,1)S(1)} %reshape.122), channel_id=1, replica_groups=mesh['member'=2,'wave'=4,'lev'=2,'fld'=2] {'lev'}, dimensions={0} | all-to-all | bytes 6291456 | tf_op jit(solution)/shard_map/all_to_all | solution.py:48
  308.7 20.4 %reshape.123 = bf16[4096,12,32]{2,1,0:T(8,128)(2,1)} reshape(bf16[2,2,393216]{2,1,0:T(2,128)(2,1)} %all_to_all.33) | data formatting | bytes 6291456
  329.1 26.0 %copy.34 = bf16[12,32,2,2048]{3,2,1,0:T(2,128)(2,1)S(1)} copy(bf16[12,32,2,2048]{1,0,3,2:T(8,128)(2,1)} %bitcast.38) | data formatting | bytes 6291456 | tf_op jit(solution)/shard_map/all_to_all | solution.py:48
  355.1 3.0 copy.32
  (26 shorter events, 0.3 us)
Async XLA Ops:
  83.7 6.7 %copy-start.15 = (s32[1024]{0:T(1024)S(1)}, s32[1024]{0:T(1024)}, u32[]{:S(2)}) copy-start(s32[1024]{0:T(1024)} %param.5) | copy-start | bytes 12292
  83.8 134.6 %all-to-all-start = ((bf16[256,2,12,128]{0,1,2,3:T(2,128)(2,1)}), bf16[256,2,12,128]{0,1,2,3:T(2,128)(2,1)S(1)}, u32[]{:S(2)}, u32[]{:S(2)}) async-start(bf16[256,2,12,128]{0,1,2,3:T(2,128)(2,1)} %copy.26), calls=%async_computation | async-start | bytes 3145728 | tf_op jit(solution)/shard_map/all_to_all | solution.py:41
  220.6 1.2 copy-start.14
  221.8 1.2 copy-start.11
  221.8 1.5 copy-start.13
  223.4 1.2 copy-start.9
  223.4 1.5 copy-start.12
  224.9 1.2 copy-start.7
  224.9 1.5 copy-start.10
  226.4 1.2 copy-start.5
  226.4 1.5 copy-start.8
  228.0 1.2 copy-start.3
  228.0 1.5 copy-start.6
  229.5 1.2 copy-start.1
  229.5 1.5 copy-start.4
  231.1 1.2 copy-start
  231.1 1.5 copy-start.2
where the time goes:
time: 364 us; the launch traced here: 358 us
  other arithmetic  167 us (46%)
  local copies, waits for them, and re-layouts  96.5 us (27%)
  matrix products  47.8 us (13%)
  blocking collectives  39.9 us (11%)
  starting transfers between devices  6.66 us (2%)
    neg x1, other arithmetic, longitude_sum(): table = jnp.concatenate([cosines, -sines], axis=0)  64.9 us
    convert_element_type x1, other arithmetic, longitude_sum(): cosines = (weights * jnp.cos(angles)).astype(jnp.bfloat16)  63 us
    unnamed x42, local copies, waits for them, and re-layouts  44.6 us
    dot_general x1, matrix products, shards(): jnp.einsum('shn,srcn->srch', mirrored, coeffs, preferred_element_type=jnp...  40 us
    all_to_all x1, blocking collectives, shards(): lax.all_to_all(row_values, 'lev', split_axis=2, concat_axis=0, tiled=True)  39.9 us
    all_to_all x2, local copies, waits for them, and re-layouts, shards(): lax.all_to_all(row_values, 'lev', split_axis=2, concat_axis=0, tiled=True)  29 us
    mul x1, other arithmetic, shards(): mirrored = jnp.concatenate([legendre, legendre * signs[:, None, :]], axis=1)  22.9 us
    concatenate x2, local copies, waits for them, and re-layouts, shards(): row_values = jnp.concatenate(pieces, axis=2)  16.2 us
  transfers between devices with their start and end apart: 1, of which 0 were waited for; matrix products, arithmetic and copies ran while one was open for 36% of the time, Pallas kernels for 0%

commit v1 on v0

v1 whole, which is shorter than its diff:
```python
import functools
import math

import jax
import jax.numpy as jnp
import numpy as np
from jax import lax
from jax.experimental import pallas as pl
from jax.experimental.pallas import tpu as pltpu
from jax.sharding import PartitionSpec as P

NLON = 4096
PAIRS = 32
GROUP = 2 * PAIRS
STEP = 16
CHUNKS = (2, 2)
MIB = 1 << 20


def pair_lists(wave_order, waves):
    blocks = wave_order.reshape(waves, -1)
    slots = blocks.shape[1]
    rank = jnp.sum((blocks[:, None, :] < blocks[:, :, None]).astype(jnp.int32), axis=2)
    places = jnp.arange(slots, dtype=jnp.int32)
    hit = rank[:, None, :] == places[None, :, None]
    order = jnp.sum(jnp.where(hit, places[None, None, :], 0), axis=2)
    lower = jnp.sum(jnp.where(hit[:, : slots // 2], blocks[:, None, :], 0), axis=2)
    return order.reshape(-1), lower.reshape(-1)


def rows_of(values_ref, first, count):
    rows = lax.broadcasted_iota(jnp.int32, (8, 128), 0)
    pieces = []
    for base in range(0, count, 8):
        piece = jnp.full((8, 128), values_ref[first + base], jnp.int32)
        for row in range(1, 8):
            piece = jnp.where(rows == row, values_ref[first + base + row], piece)
        pieces.append(piece)
    return jnp.concatenate(pieces, axis=0)


def legendre_kernel(first_group, groups, order_ref, lower_ref, spectral_ref, legendre_ref, *rest):
    waves = lax.axis_size("wave")
    out_refs = rest[:waves]
    coeffs_ref, values_ref, by_slot, turned, sems = rest[waves:]
    columns, tiles = spectral_ref.shape[1], spectral_ref.shape[2]
    rows = 8 * legendre_ref.shape[1]
    mine = lax.axis_index("wave")
    slots_here = spectral_ref.shape[0]
    group = pl.program_id(0)
    steps = PAIRS // STEP

    @pl.when(group == 0)
    def _():
        @pl.loop(0, groups * PAIRS)
        def _(p):
            rank = first_group * PAIRS + p
            low = order_ref[mine * slots_here + rank]
            high = order_ref[mine * slots_here + slots_here - 1 - rank]
            t = lower_ref[mine * (slots_here // 2) + rank] // 128
            for kind, (source, target) in enumerate(((legendre_ref, values_ref), (spectral_ref, coeffs_ref))):
                sem = sems.at[kind, p // STEP]
                pltpu.make_async_copy(
                    source.at[low, :, pl.ds(t, tiles - t)], target.at[p, :, pl.ds(0, tiles - t)], sem
                ).start()
                pltpu.make_async_copy(
                    source.at[high, :, pl.ds(tiles - 1 - t, t + 1)], target.at[p, :, pl.ds(tiles - t, t + 1)], sem
                ).start()

    lanes = lax.broadcasted_iota(jnp.int32, (STEP, 128), 1)

    @pl.loop(0, steps)
    def _(step):
        place = group * steps + step
        first = place * STEP
        wavenums = rows_of(lower_ref, mine * (slots_here // 2) + first_group * PAIRS + first, STEP)
        for kind, target in enumerate((values_ref, coeffs_ref)):
            arrived = target.at[pl.ds(first, STEP)]
            pltpu.make_async_copy(arrived, arrived, sems.at[kind, place]).wait()
        t, inside = wavenums // 128, wavenums & 127
        parity = jnp.where(((lanes + wavenums) & 1) == 1, -1.0, 1.0)
        masks = [[], [], [], []]
        for i in range(tiles + 1):
            low = t + i < tiles
            if i == 0:
                low = lanes >= inside
            high = (t + i > tiles) | ((t + i == tiles) & (lanes >= 127 - inside))
            low, high = jnp.where(low, 1.0, 0.0), jnp.where(high, 1.0, 0.0)
            for mask, value in zip(masks, (low, low * parity, high, -high * parity)):
                mask.append(value.astype(jnp.bfloat16))
        masks = [jnp.concatenate(mask, axis=1) for mask in masks]
        for s in range(STEP):
            coeffs = jnp.concatenate(
                [coeffs_ref[first + s, :, i].reshape(2 * columns, 128) for i in range(tiles + 1)], axis=1
            )
            values = jnp.concatenate([values_ref[first + s, :, i].reshape(rows, 128) for i in range(tiles + 1)], axis=1)
            left = jnp.concatenate([coeffs * mask[s : s + 1] for mask in masks], axis=0)
            sums = lax.dot_general(left, values, (((1,), (1,)), ((), ())), preferred_element_type=jnp.float32)
            by_slot[:, step * STEP + s, :] = sums[: 4 * columns]
            by_slot[:, PAIRS + step * STEP + s, :] = sums[4 * columns :]

    for pair in range(2 * columns):
        turned[pair] = jnp.concatenate([by_slot[2 * pair].T, by_slot[2 * pair + 1].T], axis=1)
    rows_dest = 2 * rows // waves
    half = waves // 2
    for shift in range(waves):
        dest = lax.rem(mine + shift, waves)
        side, block = dest // half, lax.rem(dest, half)
        piece = turned[
            pl.ds(side * columns, columns), pl.ds(pl.multiple_of(block * rows_dest, rows_dest), rows_dest), :
        ]
        out_refs[shift][0] = piece.reshape(columns * rows_dest, 2 * GROUP).astype(jnp.bfloat16)


def legendre_part(spectral, legendre, lists, first_group, groups):
    waves = lax.axis_size("wave")
    slots, columns, tiles = spectral.shape[:3]
    rows = 8 * legendre.shape[1]
    rows_dest = 2 * rows // waves
    pairs = groups * PAIRS
    shape = jax.ShapeDtypeStruct((groups, columns * rows_dest, 2 * GROUP), jnp.bfloat16)
    return pl.pallas_call(
        functools.partial(legendre_kernel, first_group, groups),
        grid_spec=pltpu.PrefetchScalarGridSpec(
            num_scalar_prefetch=2,
            grid=(groups,),
            in_specs=[pl.BlockSpec(memory_space=pl.ANY)] * 2,
            out_specs=[pl.BlockSpec((1,) + shape.shape[1:], lambda g, *_: (g, 0, 0))] * waves,
            scratch_shapes=[
                pltpu.VMEM((pairs, columns, tiles + 1, 2, 128), jnp.bfloat16),
                pltpu.VMEM((pairs, rows // 8, tiles + 1, 8, 128), jnp.bfloat16),
                pltpu.VMEM((4 * columns, GROUP, rows), jnp.float32),
                pltpu.VMEM((2 * columns, rows, 2 * GROUP), jnp.float32),
                pltpu.SemaphoreType.DMA((2, pairs // STEP)),
            ],
        ),
        out_shape=[shape] * waves,
        compiler_params=pltpu.CompilerParams(vmem_limit_bytes=56 * MIB),
        cost_estimate=pl.CostEstimate(flops=1 << 10, bytes_accessed=1 << 10, transcendentals=0),
    )(*lists, spectral, legendre)


def cos_sin(phase):
    quarter = NLON // 4
    quadrant = (phase + quarter // 2) // quarter
    x = (phase - quadrant * quarter).astype(jnp.float32) * (2.0 * math.pi / NLON)
    y = x * x
    sine = x * (1.0 + y * (-1.0 / 6 + y * (1.0 / 120 + y * (-1.0 / 5040 + y * (1.0 / 362880)))))
    cosine = 1.0 + y * (-0.5 + y * (1.0 / 24 + y * (-1.0 / 720 + y * (1.0 / 40320 + y * (-1.0 / 3628800)))))
    swap = (quadrant & 1) == 1
    c = jnp.where(swap, sine, cosine)
    s = jnp.where(swap, cosine, sine)
    c = jnp.where(((quadrant + 1) & 2) == 2, -c, c)
    s = jnp.where((quadrant & 2) == 2, -s, s)
    return c, s


def table_kernel(shifts_ref, groups_ref, lower_ref, out_ref):
    waves = lax.axis_size("wave")
    pairs_here = lower_ref.shape[0] // waves
    shift, group = shifts_ref[pl.program_id(0)], groups_ref[pl.program_id(0)]
    source = lax.rem(lax.axis_index("wave") + waves - shift, waves)
    width = out_ref.shape[1]
    lon_start = lax.axis_index("lev") * width
    lower = rows_of(lower_ref, source * pairs_here + group * PAIRS, PAIRS)
    wavenums = jnp.concatenate([lower, 2 * lower_ref.shape[0] - 1 - lower], axis=0)
    lanes = lax.broadcasted_iota(jnp.int32, (GROUP, 128), 1)
    fine_cos, fine_sin = cos_sin((wavenums * lanes) & (NLON - 1))
    coarse_cos, coarse_sin = cos_sin((wavenums * (lon_start + 128 * lanes)) & (NLON - 1))
    weight = jnp.where(wavenums == 0, 1.0, 2.0)
    coarse_cos, coarse_sin = coarse_cos * weight, coarse_sin * weight
    for box in range(width // 128):
        c, s = coarse_cos[:, box : box + 1], coarse_sin[:, box : box + 1]
        cosines = c * fine_cos - s * fine_sin
        sines = s * fine_cos + c * fine_sin
        out_ref[0:GROUP, box * 128 : (box + 1) * 128] = cosines.astype(jnp.bfloat16)
        out_ref[GROUP : 2 * GROUP, box * 128 : (box + 1) * 128] = (-sines).astype(jnp.bfloat16)


def longitude_table(lower, blocks):
    width = NLON // lax.axis_size("lev")
    shifts, groups = np.array(blocks, np.int32).T
    return pl.pallas_call(
        table_kernel,
        grid_spec=pltpu.PrefetchScalarGridSpec(
            num_scalar_prefetch=3,
            grid=(len(blocks),),
            in_specs=[],
            out_specs=pl.BlockSpec((2 * GROUP, width), lambda i, *_: (i, 0)),
        ),
        out_shape=jax.ShapeDtypeStruct((len(blocks) * 2 * GROUP, width), jnp.bfloat16),
        compiler_params=pltpu.CompilerParams(vmem_limit_bytes=16 * MIB),
        cost_estimate=pl.CostEstimate(flops=1 << 10, bytes_accessed=1 << 10, transcendentals=0),
    )(jnp.asarray(shifts), jnp.asarray(groups), lower)


def longitude_kernel(layout, n_in, last, *refs):
    in_refs, table_ref, rest = refs[:n_in], refs[n_in], refs[n_in + 1 :]
    out_ref, left = rest[-2:]
    levs = lax.axis_size("lev")
    height = left.shape[0] // levs

    @pl.when(pl.program_id(0) == 0)
    def _():
        for shift, blocks in enumerate(layout):
            for place, (operand, group) in enumerate(blocks):
                left[shift * height : (shift + 1) * height, place * 2 * GROUP : (place + 1) * 2 * GROUP] = in_refs[
                    operand
                ][group]

    for shift in range(levs):
        here = slice(shift * height, (shift + 1) * height)
        values = jnp.dot(left[here], table_ref[...], preferred_element_type=jnp.float32)
        if len(rest) == 3:
            values = values + rest[0][here]
        if last:
            lev = lax.rem(lax.axis_index("lev") + levs - shift, levs)
            out_ref[lev] = values.reshape(out_ref.shape[1:]).astype(jnp.bfloat16)
        else:
            out_ref[here] = values


def longitude_part(pieces, table, total, last, columns):
    levs = len(pieces)
    height = pieces[0][0].shape[1]
    depth, width = table.shape
    tile = min(512, width)
    operands, layout = [], []
    for row in pieces:
        blocks = []
        for piece in row:
            blocks += [(len(operands), g) for g in range(piece.shape[0])]
            operands.append(piece)
        layout.append(blocks)
    n_in = len(operands)
    specs = [pl.BlockSpec(piece.shape, lambda j: (0, 0, 0)) for piece in operands]
    operands.append(table)
    specs.append(pl.BlockSpec((depth, tile), lambda j: (0, j)))
    if total is not None:
        operands.append(total)
        specs.append(pl.BlockSpec((levs * height, tile), lambda j: (0, j)))
    if last:
        out_spec = pl.BlockSpec((levs, columns, height // columns, tile), lambda j: (0, 0, 0, j))
        out_shape = jax.ShapeDtypeStruct((levs, columns, height // columns, width), jnp.bfloat16)
    else:
        out_spec = pl.BlockSpec((levs * height, tile), lambda j: (0, j))
        out_shape = jax.ShapeDtypeStruct((levs * height, width), jnp.float32)
    return pl.pallas_call(
        functools.partial(longitude_kernel, layout, n_in, last),
        grid=(width // tile,),
        in_specs=specs,
        out_specs=out_spec,
        out_shape=out_shape,
        scratch_shapes=[pltpu.VMEM((levs * height, depth), jnp.bfloat16)],
        compiler_params=pltpu.CompilerParams(vmem_limit_bytes=32 * MIB),
        cost_estimate=pl.CostEstimate(flops=1 << 10, bytes_accessed=1 << 10, transcendentals=0),
    )(*operands)


def send(array, axis, shift):
    size = lax.axis_size(axis)
    return lax.ppermute(array, axis, [(i, (i + shift) % size) for i in range(size)])


def shards(spectral, legendre, wave_order):
    slots, parts, columns, degrees = spectral.shape
    waves, levs = lax.axis_size("wave"), lax.axis_size("lev")
    rows, tiles = legendre.shape[1], degrees // 128
    groups = slots // GROUP
    spectral = spectral.reshape(slots, parts, columns, tiles, 128).transpose(0, 2, 3, 1, 4)
    legendre = legendre.reshape(slots, rows // 8, 8, tiles, 128).transpose(0, 1, 3, 2, 4)
    order, lower = pair_lists(wave_order, waves)
    sizes = list(CHUNKS) if groups == sum(CHUNKS) else [groups]
    far_first = sorted(range(1, waves), key=lambda shift: (abs(2 * shift - waves), shift))
    blocks, arrived = {}, {}
    first_group = 0
    lists = (order, lower)
    for chunk, size in enumerate(sizes):
        outs = legendre_part(spectral, legendre, lists, first_group, size)
        lists = lax.optimization_barrier((order, lower, outs[0]))[:2]
        for shift in [0] + far_first:
            piece = outs[shift]
            if shift != 0:
                if chunk > 0:
                    before = (chunk - 1, shift)
                    piece, arrived[before] = lax.optimization_barrier((piece, arrived[before]))
                piece = send(piece, "wave", shift)
            arrived[chunk, shift] = piece
            blocks[chunk, shift] = [(shift, first_group + g) for g in range(size)]
        first_group += size
    keys = list(arrived)
    late = far_first if len(sizes) > 1 else []
    cut = [[key for key in keys if key[0] < len(sizes) - 1 or key[1] not in late]]
    if late:
        cut.append([(len(sizes) - 1, shift) for shift in late])
    pieces = {}

    def relay(key):
        before = (key[0] - 1, key[1])
        piece = arrived[key]
        if before in pieces:
            tied = lax.optimization_barrier((piece, *pieces[before]))
            piece, pieces[before] = tied[0], list(tied[1:])
        pieces[key] = [piece] + [send(piece, "lev", lev) for lev in range(1, levs)]

    final = [key for key in keys if key[0] == len(sizes) - 1 and key[1] != 0]
    for key in keys:
        if key not in final:
            relay(key)
    if len(sizes) > 1:
        first_relayed = (len(sizes) - 2, far_first[0])
        tied = lax.optimization_barrier((lists[1], *pieces[first_relayed]))
        lists, pieces[first_relayed] = (order, tied[0]), list(tied[1:])
    tables = [longitude_table(lists[1], [block for name in names for block in blocks[name]]) for names in cut]
    for key in final:
        tied = lax.optimization_barrier((arrived[key], *tables))
        arrived[key], tables = tied[0], list(tied[1:])
        relay(key)
    total = None
    for index, names in enumerate(cut):
        rows_of_pieces = [[pieces[name][lev] for name in names] for lev in range(levs)]
        total = longitude_part(rows_of_pieces, tables[index], total, index == len(cut) - 1, columns)
    return total


def solution(mesh):
    in_specs = (P(("member", "wave"), None, ("lev", "fld"), None), P("wave", None, None), P())
    out_specs = P(None, "fld", ("member", "wave"), "lev")
    return jax.shard_map(shards, mesh=mesh, in_specs=in_specs, out_specs=out_specs, check_vma=False)
```

time: 364 us -> 76.8 us (0.21); the launches traced: 358 us -> 76.6 us
  other arithmetic: 167 us -> 1.48 us
  local copies, waits for them, and re-layouts: 96.5 us -> 1.32 us
  matrix products: 47.8 us -> 0 us
  Pallas kernels: 0 us -> 44.6 us
  blocking collectives: 39.9 us -> 0 us
  starting transfers between devices: 6.66 us -> 19.8 us
  waiting for transfers between devices: 0.01 us -> 9.18 us
    neg x1 -> x0, other arithmetic: 64.9 us -> none  [longitude_sum(): table = jnp.concatenate([cosines, -sines], axis=0)]
    convert_element_type x2 -> x0, other arithmetic: 63.7 us -> none  [the longest x1 63 us: longitude_sum(): cosines = (weights * jnp.cos(angles)).astype(jnp.bfloat16)]
    dot_general x9 -> x0, matrix products: 47.8 us -> none  [the longest x1 40 us: shards(): jnp.einsum('shn,srcn->srch', mirrored, coeffs, preferred_element_type=jnp...]
    pallas_call x0 -> x6, Pallas kernels: none -> 44.6 us  [the longest x2 25.2 us: legendre_part(): pl.pallas_call(functools.partial(legendre_kernel, first_group, groups), g...]
    unnamed x42 -> x15, local copies, waits for them, and re-layouts: 44.6 us -> 0.63 us
    all_to_all x1 -> x0, blocking collectives: 39.9 us -> none  [shards(): lax.all_to_all(row_values, 'lev', split_axis=2, concat_axis=0, tiled=True)]
    all_to_all x4 -> x0, local copies, waits for them, and re-layouts: 29.5 us -> none  [the longest x2 29 us: shards(): lax.all_to_all(row_values, 'lev', split_axis=2, concat_axis=0, tiled=True)]
    mul x1 -> x0, other arithmetic: 22.9 us -> none  [shards(): mirrored = jnp.concatenate([legendre, legendre * signs[:, None, :]], axis=1)]
  transfers between devices with their start and end apart: 1 -> 14, of which waited for: 0 -> 4; matrix products, arithmetic and copies ran while one was open for 36% -> 0% of each run, Pallas kernels for 0% -> 35%
where the time goes in v1:
time: 76.8 us; the launch traced here: 76.6 us
  Pallas kernels  44.6 us (58%)
  starting transfers between devices  19.8 us (26%)
  waiting for transfers between devices  9.18 us (12%)
  other arithmetic  1.48 us (2%)
  local copies, waits for them, and re-layouts  1.32 us (2%)
    pallas_call x2, Pallas kernels, legendre_part(): pl.pallas_call(functools.partial(legendre_kernel, first_group, groups), g...  25.2 us
    ppermute x14, starting transfers between devices, send(): lax.ppermute(array, axis, [(i, (i + shift) % size) for i in range(size)])  19.8 us
    pallas_call x2, Pallas kernels, longitude_part(): pl.pallas_call(functools.partial(longitude_kernel, layout, n_in, last), g...  10.8 us
    ppermute x14, waiting for transfers between devices, send(): lax.ppermute(array, axis, [(i, (i + shift) % size) for i in range(size)])  9.18 us
    pallas_call x2, Pallas kernels, longitude_table(): pl.pallas_call(table_kernel, grid_spec=pltpu.PrefetchScalarGridSpec(num_s...  8.63 us
  transfers between devices with their start and end apart: 14, of which 4 were waited for; matrix products, arithmetic and copies ran while one was open for 0% of the time, Pallas kernels for 35%

profile of v1, /device:TPU:0, one launch (start us, length us, event | category | flops | bytes accessed | tf_op | source)
XLA Modules:
  0.0 76.6 jit_solution(9137906787160555417)
XLA Ops:
  0.0 0.7 lt.15
  0.7 0.4 convert_reduce_fusion
  1.1 0.2 select_reduce_fusion
  1.3 0.1 iota_compare_fusion
  1.5 0.6 copy.8
  2.1 0.7 select_reduce_fusion.1
  2.8 12.7 %shard_map.73 = (bf16[2,384,128]{2,1,0:T(8,128)(2,1)}, bf16[2,384,128]{2,1,0:T(8,128)(2,1)}, bf16[2,384,128]{2,1,0:T(8,128)(2,1)}, bf16[2,384,128]{2,1,0:T(8,128)(2,1)}) custom-call(s32[1024]{0:T(1024)} %bitcast.17, s32[512]{0:T(512)} %bitcast.9, bf16[256,12,8,2,128]{4,3,2,1,0:T(2,128)(2,1)} %bitcast.15, bf16[256,8,8,8,128]{4,3,2,1,0:T(8,128)(2,1)} %bitcast.13), custom_call_target="tpu_custom_call" | custom-call | flops 1024 | bytes 1024 | tf_op jit(solution)/shard_map/pallas_call | solution.py:122
  15.5 4.1 %collective-permute-start = (bf16[2,384,128]{2,1,0:T(8,128)(2,1)}, bf16[2,384,128]{2,1,0:T(8,128)(2,1)S(1)}, u32[]{:S(2)}, u32[]{:S(2)}) collective-permute-start(bf16[2,384,128]{2,1,0:T(8,128)(2,1)} %get-tuple-element.50), channel_id=1, source_target_pairs={{0,8},{4,12},{8,0},{12,4},{1,9},{5,13},{9,1},{13,5},{2,10},{6,14},... | collective-permute-start | bytes 589832 | tf_op jit(solution)/shard_map/ppermute | solution.py:262
  19.6 1.6 %collective-permute-start.3 = (bf16[2,384,128]{2,1,0:T(8,128)(2,1)}, bf16[2,384,128]{2,1,0:T(8,128)(2,1)S(1)}, u32[]{:S(2)}, u32[]{:S(2)}) collective-permute-start(bf16[2,384,128]{2,1,0:T(8,128)(2,1)} %get-tuple-element.61), channel_id=1, source_target_pairs={{0,4},{4,8},{8,12},{12,0},{1,5},{5,9},{9,13},{13,1},{2,6},{6,10},{... | collective-permute-start | bytes 589832 | tf_op jit(solution)/shard_map/ppermute | solution.py:262
  21.1 2.3 %collective-permute-start.6 = (bf16[2,384,128]{2,1,0:T(8,128)(2,1)}, bf16[2,384,128]{2,1,0:T(8,128)(2,1)S(1)}, u32[]{:S(2)}, u32[]{:S(2)}) collective-permute-start(bf16[2,384,128]{2,1,0:T(8,128)(2,1)} %get-tuple-element.69), channel_id=1, source_target_pairs={{0,12},{4,0},{8,4},{12,8},{1,13},{5,1},{9,5},{13,9},{2,14},{6,2},{... | collective-permute-start | bytes 589832 | tf_op jit(solution)/shard_map/ppermute | solution.py:262
  23.4 0.0 copy-start.6
  23.4 1.6 %collective-permute-start.12 = (bf16[2,384,128]{2,1,0:T(8,128)(2,1)}, bf16[2,384,128]{2,1,0:T(8,128)(2,1)S(1)}, u32[]{:S(2)}, u32[]{:S(2)}) collective-permute-start(bf16[2,384,128]{2,1,0:T(8,128)(2,1)} %get-tuple-element.77.refs_0_), channel_id=1, source_target_pairs={{0,2},{2,0},{1,3},{3,1},{4,6},{6,4},{5,7},{7,5},{8,10},{10,8},{9,1... | collective-permute-start | bytes 589832 | tf_op jit(solution)/shard_map/ppermute | solution.py:262
  25.0 12.5 %shard_map.74 = (bf16[2,384,128]{2,1,0:T(8,128)(2,1)}, bf16[2,384,128]{2,1,0:T(8,128)(2,1)}, bf16[2,384,128]{2,1,0:T(8,128)(2,1)}, bf16[2,384,128]{2,1,0:T(8,128)(2,1)}) custom-call(s32[1024]{0:T(1024)} %bitcast.18, s32[512]{0:T(512)} %bitcast.10, bf16[256,12,8,2,128]{4,3,2,1,0:T(2,128)(2,1)} %bitcast.16, bf16[256,8,8,8,128]{4,3,2,1,0:T(8,128)(2,1)} %bitcast.14), custom_call_target="tpu_custom_call" | custom-call | flops 1024 | bytes 1024 | tf_op jit(solution)/shard_map/pallas_call | solution.py:122
  37.5 0.0 copy-start.1
  37.5 0.0 copy-start
  37.5 0.0 collective-permute-done.refs_1_
  37.5 0.6 collective-permute-start.2
  38.2 0.0 collective-permute-start.1
  38.2 0.0 collective-permute-done.3.refs_2_
  38.2 0.6 collective-permute-start.4
  38.7 0.0 collective-permute-done.6.refs_3_
  38.7 1.5 %collective-permute-start.5 = (bf16[2,384,128]{2,1,0:T(8,128)(2,1)S(1)}, bf16[2,384,128]{2,1,0:T(8,128)(2,1)S(1)}, u32[]{:S(2)}, u32[]{:S(2)}) collective-permute-start(bf16[2,384,128]{2,1,0:T(8,128)(2,1)S(1)} %collective-permute-done.3.refs_2_), channel_id=1, source_target_pairs={{0,2},{2,0},{1,3},{3,1},{4,6},{6,4},{5,7},{7,5},{8,10},{10,8},{9,1... | collective-permute-start | bytes 589832 | tf_op jit(solution)/shard_map/ppermute | solution.py:262
  40.2 0.0 collective-permute-done.12.refs_5_
  40.2 3.2 %collective-permute-start.7 = (bf16[2,384,128]{2,1,0:T(8,128)(2,1)}, bf16[2,384,128]{2,1,0:T(8,128)(2,1)S(1)}, u32[]{:S(2)}, u32[]{:S(2)}) collective-permute-start(bf16[2,384,128]{2,1,0:T(8,128)(2,1)} %get-tuple-element.70), channel_id=1, source_target_pairs={{0,12},{4,0},{8,4},{12,8},{1,13},{5,1},{9,5},{13,9},{2,14},{6,2},{... | collective-permute-start | bytes 589832 | tf_op jit(solution)/shard_map/ppermute | solution.py:262
  43.5 2.0 %collective-permute-done.2.refs_6_ = bf16[2,384,128]{2,1,0:T(8,128)(2,1)S(1)} collective-permute-done((bf16[2,384,128]{2,1,0:T(8,128)(2,1)S(1)}, bf16[2,384,128]{2,1,0:T(8,128)(2,1)S(1)}, u32[]{:S(2)}, u32[]{:S(2)}) %collective-permute-start.2) | collective-permute-done | bytes 196640 | tf_op jit(solution)/shard_map/ppermute | solution.py:262
  45.5 0.2 collective-permute-start.8
  45.7 0.0 copy-done.2
  45.7 0.0 copy-done.3
  45.7 0.0 copy-done.4
  45.7 3.4 %shard_map.76.refs_6_ = bf16[768,2048]{1,0:T(8,128)(2,1)S(1)} custom-call(s32[6]{0:T(128)S(1)} %copy-done.4, s32[6]{0:T(128)S(1)} %copy-done.3, s32[512]{0:T(512)S(1)} %bitcast.11), custom_call_target="tpu_custom_call" | custom-call | flops 1024 | bytes 1024 | tf_op jit(solution)/shard_map/pallas_call | solution.py:183
  49.1 0.0 copy-done.5
  49.1 0.0 copy-done.6
  49.1 5.2 %shard_map.75.refs_10_ = bf16[1280,2048]{1,0:T(8,128)(2,1)S(1)} custom-call(s32[10]{0:T(128)S(1)} %copy-done.6, s32[10]{0:T(128)S(1)} %copy-done.5, s32[512]{0:T(512)S(1)} %bitcast.12), custom_call_target="tpu_custom_call" | custom-call | flops 1024 | bytes 1024 | tf_op jit(solution)/shard_map/pallas_call | solution.py:183
  54.3 0.0 collective-permute-done.1.refs_0_
  54.4 1.9 %collective-permute-start.13 = (bf16[2,384,128]{2,1,0:T(8,128)(2,1)S(1)}, bf16[2,384,128]{2,1,0:T(8,128)(2,1)S(1)}, u32[]{:S(2)}, u32[]{:S(2)}) collective-permute-start(bf16[2,384,128]{2,1,0:T(8,128)(2,1)S(1)} %copy-done.1), channel_id=1, source_target_pairs={{0,2},{2,0},{1,3},{3,1},{4,6},{6,4},{5,7},{7,5},{8,10},{10,8},{9,1... | collective-permute-start | bytes 589832 | tf_op jit(solution)/shard_map/ppermute | solution.py:262
  56.2 0.0 collective-permute-done.4.refs_1_
  56.2 0.0 collective-permute-done.5.refs_7_
  56.2 0.0 collective-permute-done.7.refs_2_
  56.3 0.0 collective-permute-done.8.refs_8_
  56.3 0.3 collective-permute-start.11
  56.5 1.8 %collective-permute-start.10 = (bf16[2,384,128]{2,1,0:T(8,128)(2,1)S(1)}, bf16[2,384,128]{2,1,0:T(8,128)(2,1)S(1)}, u32[]{:S(2)}, u32[]{:S(2)}) collective-permute-start(bf16[2,384,128]{2,1,0:T(8,128)(2,1)S(1)} %collective-permute-done.4.refs_1_), channel_id=1, source_target_pairs={{0,2},{2,0},{1,3},{3,1},{4,6},{6,4},{5,7},{7,5},{8,10},{10,8},{9,1... | collective-permute-start | bytes 589832 | tf_op jit(solution)/shard_map/ppermute | solution.py:262
  58.4 0.2 collective-permute-start.9
  58.6 3.7 %collective-permute-done.13.refs_9_ = bf16[2,384,128]{2,1,0:T(8,128)(2,1)S(1)} collective-permute-done((bf16[2,384,128]{2,1,0:T(8,128)(2,1)S(1)}, bf16[2,384,128]{2,1,0:T(8,128)(2,1)S(1)}, u32[]{:S(2)}, u32[]{:S(2)}) %collective-permute-start.13) | collective-permute-done | bytes 196640 | tf_op jit(solution)/shard_map/ppermute | solution.py:262
  62.3 5.9 %shard_map.77.refs_7_ = f32[768,2048]{1,0:T(8,128)S(1)} custom-call(bf16[2,384,128]{2,1,0:T(8,128)(2,1)S(1)} %copy-done, bf16[2,384,128]{2,1,0:T(8,128)(2,1)S(1)} %collective-permute-done.refs_1_, bf16[2,384,128]{2,1,0:T(8,128)(2,1)S(1)} %collective-permute-done.3.refs_2_, bf16[2,384,128]{2,1,0:T(8,128)(2,1)S(1)} %collective-permute-done.6.refs_3_, ...), custom_call_target="tpu_custom_call" | custom-call | flops 1024 | bytes 1024 | tf_op jit(solution)/shard_map/pallas_call | solution.py:248
  68.2 0.0 collective-permute-done.11.refs_5_
  68.2 1.4 %collective-permute-done.10.refs_4_ = bf16[2,384,128]{2,1,0:T(8,128)(2,1)S(1)} collective-permute-done((bf16[2,384,128]{2,1,0:T(8,128)(2,1)S(1)}, bf16[2,384,128]{2,1,0:T(8,128)(2,1)S(1)}, u32[]{:S(2)}, u32[]{:S(2)}) %collective-permute-start.10) | collective-permute-done | bytes 196640 | tf_op jit(solution)/shard_map/ppermute | solution.py:262
  69.6 2.1 %collective-permute-done.9.refs_3_ = bf16[2,384,128]{2,1,0:T(8,128)(2,1)S(1)} collective-permute-done((bf16[2,384,128]{2,1,0:T(8,128)(2,1)S(1)}, bf16[2,384,128]{2,1,0:T(8,128)(2,1)S(1)}, u32[]{:S(2)}, u32[]{:S(2)}) %collective-permute-start.9) | collective-permute-done | bytes 196640 | tf_op jit(solution)/shard_map/ppermute | solution.py:262
  71.7 4.9 %shard_map.78 = bf16[2,12,32,2048]{3,2,1,0:T(8,128)(2,1)} custom-call(bf16[2,384,128]{2,1,0:T(8,128)(2,1)S(1)} %collective-permute-done.1.refs_0_, bf16[2,384,128]{2,1,0:T(8,128)(2,1)S(1)} %collective-permute-done.4.refs_1_, bf16[2,384,128]{2,1,0:T(8,128)(2,1)S(1)} %collective-permute-done.7.refs_2_, ...), custom_call_target="tpu_custom_call" | custom-call | flops 1024 | bytes 1024 | tf_op jit(solution)/shard_map/pallas_call | solution.py:248
  (6 shorter events, 0.0 us)
Async XLA Ops:
  15.5 22.1 %collective-permute-start = (bf16[2,384,128]{2,1,0:T(8,128)(2,1)}, bf16[2,384,128]{2,1,0:T(8,128)(2,1)S(1)}, u32[]{:S(2)}, u32[]{:S(2)}) collective-permute-start(bf16[2,384,128]{2,1,0:T(8,128)(2,1)} %get-tuple-element.50), channel_id=1, source_target_pairs={{0,8},{4,12},{8,0},{12,4},{1,9},{5,13},{9,1},{13,5},{2,10},{6,14},... | collective-permute-start | bytes 589832 | tf_op jit(solution)/shard_map/ppermute | solution.py:262
  19.6 18.6 %collective-permute-start.3 = (bf16[2,384,128]{2,1,0:T(8,128)(2,1)}, bf16[2,384,128]{2,1,0:T(8,128)(2,1)S(1)}, u32[]{:S(2)}, u32[]{:S(2)}) collective-permute-start(bf16[2,384,128]{2,1,0:T(8,128)(2,1)} %get-tuple-element.61), channel_id=1, source_target_pairs={{0,4},{4,8},{8,12},{12,0},{1,5},{5,9},{9,13},{13,1},{2,6},{6,10},{... | collective-permute-start | bytes 589832 | tf_op jit(solution)/shard_map/ppermute | solution.py:262
  21.1 17.6 %collective-permute-start.6 = (bf16[2,384,128]{2,1,0:T(8,128)(2,1)}, bf16[2,384,128]{2,1,0:T(8,128)(2,1)S(1)}, u32[]{:S(2)}, u32[]{:S(2)}) collective-permute-start(bf16[2,384,128]{2,1,0:T(8,128)(2,1)} %get-tuple-element.69), channel_id=1, source_target_pairs={{0,12},{4,0},{8,4},{12,8},{1,13},{5,1},{9,5},{13,9},{2,14},{6,2},{... | collective-permute-start | bytes 589832 | tf_op jit(solution)/shard_map/ppermute | solution.py:262
  23.4 22.3 %copy-start.2 = (s32[4,128]{1,0:T(4,128)S(1)}, s32[4,128]{1,0:T(4,128)}, u32[]{:S(2)}) copy-start(s32[4,128]{1,0:T(4,128)} %select_reduce_fusion.1) | copy-start | bytes 6148
  23.4 22.3 %copy-start.3 = (s32[6]{0:T(128)S(1)}, s32[6]{0:T(128)}, u32[]{:S(2)}) copy-start(s32[6]{0:T(128)} %constant.13.clone.groups_ref) | copy-start | bytes 76
  23.4 22.3 %copy-start.4 = (s32[6]{0:T(128)S(1)}, s32[6]{0:T(128)}, u32[]{:S(2)}) copy-start(s32[6]{0:T(128)} %constant.12.clone.shifts_ref) | copy-start | bytes 76
  23.4 25.7 %copy-start.5 = (s32[10]{0:T(128)S(1)}, s32[10]{0:T(128)}, u32[]{:S(2)}) copy-start(s32[10]{0:T(128)} %constant.11.clone.groups_ref) | copy-start | bytes 124
  23.4 25.7 %copy-start.6 = (s32[10]{0:T(128)S(1)}, s32[10]{0:T(128)}, u32[]{:S(2)}) copy-start(s32[10]{0:T(128)} %constant.10.clone.shifts_ref) | copy-start | bytes 124
  23.4 16.8 %collective-permute-start.12 = (bf16[2,384,128]{2,1,0:T(8,128)(2,1)}, bf16[2,384,128]{2,1,0:T(8,128)(2,1)S(1)}, u32[]{:S(2)}, u32[]{:S(2)}) collective-permute-start(bf16[2,384,128]{2,1,0:T(8,128)(2,1)} %get-tuple-element.77.refs_0_), channel_id=1, source_target_pairs={{0,2},{2,0},{1,3},{3,1},{4,6},{6,4},{5,7},{7,5},{8,10},{10,8},{9,1... | collective-permute-start | bytes 589832 | tf_op jit(solution)/shard_map/ppermute | solution.py:262
  37.5 16.8 %copy-start.1 = (bf16[2,384,128]{2,1,0:T(8,128)(2,1)S(1)}, bf16[2,384,128]{2,1,0:T(8,128)(2,1)}, u32[]{:S(2)}) copy-start(bf16[2,384,128]{2,1,0:T(8,128)(2,1)} %get-tuple-element.81.refs_4_) | copy-start | bytes 589828
  37.5 24.7 %copy-start = (bf16[2,384,128]{2,1,0:T(8,128)(2,1)S(1)}, bf16[2,384,128]{2,1,0:T(8,128)(2,1)}, u32[]{:S(2)}) copy-start(bf16[2,384,128]{2,1,0:T(8,128)(2,1)} %get-tuple-element.77.refs_0_) | copy-start | bytes 589828
  37.5 7.9 %collective-permute-start.2 = (bf16[2,384,128]{2,1,0:T(8,128)(2,1)S(1)}, bf16[2,384,128]{2,1,0:T(8,128)(2,1)S(1)}, u32[]{:S(2)}, u32[]{:S(2)}) collective-permute-start(bf16[2,384,128]{2,1,0:T(8,128)(2,1)S(1)} %collective-permute-done.refs_1_), channel_id=1, source_target_pairs={{0,2},{2,0},{1,3},{3,1},{4,6},{6,4},{5,7},{7,5},{8,10},{10,8},{9,1... | collective-permute-start | bytes 589832 | tf_op jit(solution)/shard_map/ppermute | solution.py:262
  38.2 16.2 %collective-permute-start.1 = (bf16[2,384,128]{2,1,0:T(8,128)(2,1)}, bf16[2,384,128]{2,1,0:T(8,128)(2,1)S(1)}, u32[]{:S(2)}, u32[]{:S(2)}) collective-permute-start(bf16[2,384,128]{2,1,0:T(8,128)(2,1)} %get-tuple-element.51), channel_id=1, source_target_pairs={{0,8},{4,12},{8,0},{12,4},{1,9},{5,13},{9,1},{13,5},{2,10},{6,14},... | collective-permute-start | bytes 589832 | tf_op jit(solution)/shard_map/ppermute | solution.py:262
  38.2 18.1 %collective-permute-start.4 = (bf16[2,384,128]{2,1,0:T(8,128)(2,1)}, bf16[2,384,128]{2,1,0:T(8,128)(2,1)S(1)}, u32[]{:S(2)}, u32[]{:S(2)}) collective-permute-start(bf16[2,384,128]{2,1,0:T(8,128)(2,1)} %get-tuple-element.62), channel_id=1, source_target_pairs={{0,4},{4,8},{8,12},{12,0},{1,5},{5,9},{9,13},{13,1},{2,6},{6,10},{... | collective-permute-start | bytes 589832 | tf_op jit(solution)/shard_map/ppermute | solution.py:262
  38.7 17.5 %collective-permute-start.5 = (bf16[2,384,128]{2,1,0:T(8,128)(2,1)S(1)}, bf16[2,384,128]{2,1,0:T(8,128)(2,1)S(1)}, u32[]{:S(2)}, u32[]{:S(2)}) collective-permute-start(bf16[2,384,128]{2,1,0:T(8,128)(2,1)S(1)} %collective-permute-done.3.refs_2_), channel_id=1, source_target_pairs={{0,2},{2,0},{1,3},{3,1},{4,6},{6,4},{5,7},{7,5},{8,10},{10,8},{9,1... | collective-permute-start | bytes 589832 | tf_op jit(solution)/shard_map/ppermute | solution.py:262
  40.2 16.0 %collective-permute-start.7 = (bf16[2,384,128]{2,1,0:T(8,128)(2,1)}, bf16[2,384,128]{2,1,0:T(8,128)(2,1)S(1)}, u32[]{:S(2)}, u32[]{:S(2)}) collective-permute-start(bf16[2,384,128]{2,1,0:T(8,128)(2,1)} %get-tuple-element.70), channel_id=1, source_target_pairs={{0,12},{4,0},{8,4},{12,8},{1,13},{5,1},{9,5},{13,9},{2,14},{6,2},{... | collective-permute-start | bytes 589832 | tf_op jit(solution)/shard_map/ppermute | solution.py:262
  45.5 10.8 %collective-permute-start.8 = (bf16[2,384,128]{2,1,0:T(8,128)(2,1)S(1)}, bf16[2,384,128]{2,1,0:T(8,128)(2,1)S(1)}, u32[]{:S(2)}, u32[]{:S(2)}) collective-permute-start(bf16[2,384,128]{2,1,0:T(8,128)(2,1)S(1)} %collective-permute-done.6.refs_3_), channel_id=1, source_target_pairs={{0,2},{2,0},{1,3},{3,1},{4,6},{6,4},{5,7},{7,5},{8,10},{10,8},{9,1... | collective-permute-start | bytes 589832 | tf_op jit(solution)/shard_map/ppermute | solution.py:262
  54.4 7.9 %collective-permute-start.13 = (bf16[2,384,128]{2,1,0:T(8,128)(2,1)S(1)}, bf16[2,384,128]{2,1,0:T(8,128)(2,1)S(1)}, u32[]{:S(2)}, u32[]{:S(2)}) collective-permute-start(bf16[2,384,128]{2,1,0:T(8,128)(2,1)S(1)} %copy-done.1), channel_id=1, source_target_pairs={{0,2},{2,0},{1,3},{3,1},{4,6},{6,4},{5,7},{7,5},{8,10},{10,8},{9,1... | collective-permute-start | bytes 589832 | tf_op jit(solution)/shard_map/ppermute | solution.py:262
  56.3 11.9 %collective-permute-start.11 = (bf16[2,384,128]{2,1,0:T(8,128)(2,1)S(1)}, bf16[2,384,128]{2,1,0:T(8,128)(2,1)S(1)}, u32[]{:S(2)}, u32[]{:S(2)}) collective-permute-start(bf16[2,384,128]{2,1,0:T(8,128)(2,1)S(1)} %collective-permute-done.7.refs_2_), channel_id=1, source_target_pairs={{0,2},{2,0},{1,3},{3,1},{4,6},{6,4},{5,7},{7,5},{8,10},{10,8},{9,1... | collective-permute-start | bytes 589832 | tf_op jit(solution)/shard_map/ppermute | solution.py:262
  56.5 13.0 %collective-permute-start.10 = (bf16[2,384,128]{2,1,0:T(8,128)(2,1)S(1)}, bf16[2,384,128]{2,1,0:T(8,128)(2,1)S(1)}, u32[]{:S(2)}, u32[]{:S(2)}) collective-permute-start(bf16[2,384,128]{2,1,0:T(8,128)(2,1)S(1)} %collective-permute-done.4.refs_1_), channel_id=1, source_target_pairs={{0,2},{2,0},{1,3},{3,1},{4,6},{6,4},{5,7},{7,5},{8,10},{10,8},{9,1... | collective-permute-start | bytes 589832 | tf_op jit(solution)/shard_map/ppermute | solution.py:262
  58.4 13.3 %collective-permute-start.9 = (bf16[2,384,128]{2,1,0:T(8,128)(2,1)S(1)}, bf16[2,384,128]{2,1,0:T(8,128)(2,1)S(1)}, u32[]{:S(2)}, u32[]{:S(2)}) collective-permute-start(bf16[2,384,128]{2,1,0:T(8,128)(2,1)S(1)} %collective-permute-done.1.refs_0_), channel_id=1, source_target_pairs={{0,2},{2,0},{1,3},{3,1},{4,6},{6,4},{5,7},{7,5},{8,10},{10,8},{9,1... | collective-permute-start | bytes 589832 | tf_op jit(solution)/shard_map/ppermute | solution.py:262

commit v2 on v1

--- a/solution.py
+++ b/solution.py
@@ -52,7 +52,7 @@
 
     @pl.when(group == 0)
     def _():
-        @pl.loop(0, groups * PAIRS)
+        @pl.loop(0, groups * PAIRS, unroll=4)
         def _(p):
             rank = first_group * PAIRS + p
             low = order_ref[mine * slots_here + rank]
@@ -79,28 +79,41 @@
             pltpu.make_async_copy(arrived, arrived, sems.at[kind, place]).wait()
         t, inside = wavenums // 128, wavenums & 127
         parity = jnp.where(((lanes + wavenums) & 1) == 1, -1.0, 1.0)
-        masks = [[], [], [], []]
+        always = tiles // 2 + 1
+        low_keep, low_sign, high_keep, high_sign = [], [], [], []
         for i in range(tiles + 1):
-            low = t + i < tiles
             if i == 0:
-                low = lanes >= inside
-            high = (t + i > tiles) | ((t + i == tiles) & (lanes >= 127 - inside))
-            low, high = jnp.where(low, 1.0, 0.0), jnp.where(high, 1.0, 0.0)
-            for mask, value in zip(masks, (low, low * parity, high, -high * parity)):
-                mask.append(value.astype(jnp.bfloat16))
-        masks = [jnp.concatenate(mask, axis=1) for mask in masks]
+                low = jnp.where(lanes >= inside, 1.0, 0.0)
+            else:
+                low = jnp.where(t + i < tiles, 1.0, 0.0)
+            high = jnp.where((t + i > tiles) | ((t + i == tiles) & (lanes >= 127 - inside)), 1.0, 0.0)
+            if i < tiles:
+                low_keep.append(low.astype(jnp.bfloat16))
+                low_sign.append((low * parity).astype(jnp.bfloat16))
+            if i >= always:
+                high_keep.append(high.astype(jnp.bfloat16))
+                high_sign.append((-high * parity).astype(jnp.bfloat16))
+        low_keep, low_sign, high_keep, high_sign = [
+            jnp.concatenate(mask, axis=1) for mask in (low_keep, low_sign, high_keep, high_sign)
+        ]
         for s in range(STEP):
+            row = slice(s, s + 1)
             coeffs = jnp.concatenate(
                 [coeffs_ref[first + s, :, i].reshape(2 * columns, 128) for i in range(tiles + 1)], axis=1
             )
             values = jnp.concatenate([values_ref[first + s, :, i].reshape(rows, 128) for i in range(tiles + 1)], axis=1)
-            left = jnp.concatenate([coeffs * mask[s : s + 1] for mask in masks], axis=0)
-            sums = lax.dot_general(left, values, (((1,), (1,)), ((), ())), preferred_element_type=jnp.float32)
-            by_slot[:, step * STEP + s, :] = sums[: 4 * columns]
-            by_slot[:, PAIRS + step * STEP + s, :] = sums[4 * columns :]
+            for place, part, keep, sign in (
+                (step * STEP + s, slice(0, tiles * 128), low_keep, low_sign),
+                (PAIRS + step * STEP + s, slice(always * 128, (tiles + 1) * 128), high_keep, high_sign),
+            ):
+                left = jnp.concatenate([coeffs[:, part] * keep[row], coeffs[:, part] * sign[row]], axis=0)
+                by_slot[:, place, :] = lax.dot_general(
+                    left, values[:, part], (((1,), (1,)), ((), ())), preferred_element_type=jnp.float32
+                )
 
     for pair in range(2 * columns):
-        turned[pair] = jnp.concatenate([by_slot[2 * pair].T, by_slot[2 * pair + 1].T], axis=1)
+        both = jnp.concatenate([by_slot[2 * pair], by_slot[2 * pair + 1]], axis=0)
+        turned[pair] = both.astype(jnp.bfloat16).T.astype(turned.dtype)
     rows_dest = 2 * rows // waves
     half = waves // 2
     for shift in range(waves):
@@ -289,10 +302,10 @@
             blocks[chunk, shift] = [(shift, first_group + g) for g in range(size)]
         first_group += size
     keys = list(arrived)
-    late = far_first if len(sizes) > 1 else []
-    cut = [[key for key in keys if key[0] < len(sizes) - 1 or key[1] not in late]]
-    if late:
-        cut.append([(len(sizes) - 1, shift) for shift in late])
+    late = []
+    if len(sizes) > 1:
+        late = [(len(sizes) - 1, shift) for shift in far_first]
+    cut = [names for names in ([key for key in keys if key not in late], late) if names]
     pieces = {}
 
     def relay(key):

time: 76.8 us -> 74.1 us (0.965)
  Pallas kernels: 44.6 us -> 38.9 us
  starting transfers between devices: 19.8 us -> 23.5 us
    pallas_call x2, Pallas kernels: 25.2 us -> 19.5 us  [legendre_part(): pl.pallas_call(functools.partial(legendre_kernel, first_group, groups), g...]
    ppermute x14, starting transfers between devices: 19.8 us -> 23.5 us  [send(): lax.ppermute(array, axis, [(i, (i + shift) % size) for i in range(size)])]
  transfers between devices with their start and end apart: 14 -> 14, of which waited for: 4 -> 3; matrix products, arithmetic and copies ran while one was open for 0% -> 0% of each run, Pallas kernels for 35% -> 33%
where the time goes in v2:
time: 74.1 us; the launch traced here: 73.9 us
  Pallas kernels  38.9 us (52%)
  starting transfers between devices  23.5 us (32%)
  waiting for transfers between devices  8.51 us (11%)
  other arithmetic  1.48 us (2%)
  local copies, waits for them, and re-layouts  1.32 us (2%)
    ppermute x14, starting transfers between devices, send(): lax.ppermute(array, axis, [(i, (i + shift) % size) for i in range(size)])  23.5 us
    pallas_call x2, Pallas kernels, legendre_part(): pl.pallas_call(functools.partial(legendre_kernel, first_group, groups), g...  19.5 us
    pallas_call x2, Pallas kernels, longitude_part(): pl.pallas_call(functools.partial(longitude_kernel, layout, n_in, last), g...  10.8 us
    pallas_call x2, Pallas kernels, longitude_table(): pl.pallas_call(table_kernel, grid_spec=pltpu.PrefetchScalarGridSpec(num_s...  8.63 us
    ppermute x14, waiting for transfers between devices, send(): lax.ppermute(array, axis, [(i, (i + shift) % size) for i in range(size)])  8.51 us
  transfers between devices with their start and end apart: 14, of which 3 were waited for; matrix products, arithmetic and copies ran while one was open for 0% of the time, Pallas kernels for 33%

profile of v2, /device:TPU:0, one launch (start us, length us, event | category | flops | bytes accessed | tf_op | source)
XLA Modules:
  0.0 73.9 jit_solution(11519977155240793873)
XLA Ops:
  0.0 0.7 lt.15
  0.7 0.4 convert_reduce_fusion
  1.1 0.2 select_reduce_fusion
  1.3 0.1 iota_compare_fusion
  1.5 0.6 copy.8
  2.1 0.7 select_reduce_fusion.1
  2.8 9.8 %shard_map.73 = (bf16[2,384,128]{2,1,0:T(8,128)(2,1)}, bf16[2,384,128]{2,1,0:T(8,128)(2,1)}, bf16[2,384,128]{2,1,0:T(8,128)(2,1)}, bf16[2,384,128]{2,1,0:T(8,128)(2,1)}) custom-call(s32[1024]{0:T(1024)} %bitcast.17, s32[512]{0:T(512)} %bitcast.9, bf16[256,12,8,2,128]{4,3,2,1,0:T(2,128)(2,1)} %bitcast.15, bf16[256,8,8,8,128]{4,3,2,1,0:T(8,128)(2,1)} %bitcast.13), custom_call_target="tpu_custom_call" | custom-call | flops 1024 | bytes 1024 | tf_op jit(solution)/shard_map/pallas_call | solution.py:135
  12.6 4.1 %collective-permute-start = (bf16[2,384,128]{2,1,0:T(8,128)(2,1)}, bf16[2,384,128]{2,1,0:T(8,128)(2,1)S(1)}, u32[]{:S(2)}, u32[]{:S(2)}) collective-permute-start(bf16[2,384,128]{2,1,0:T(8,128)(2,1)} %get-tuple-element.50), channel_id=1, source_target_pairs={{0,8},{4,12},{8,0},{12,4},{1,9},{5,13},{9,1},{13,5},{2,10},{6,14},... | collective-permute-start | bytes 589832 | tf_op jit(solution)/shard_map/ppermute | solution.py:275
  16.7 1.6 %collective-permute-start.3 = (bf16[2,384,128]{2,1,0:T(8,128)(2,1)}, bf16[2,384,128]{2,1,0:T(8,128)(2,1)S(1)}, u32[]{:S(2)}, u32[]{:S(2)}) collective-permute-start(bf16[2,384,128]{2,1,0:T(8,128)(2,1)} %get-tuple-element.61), channel_id=1, source_target_pairs={{0,4},{4,8},{8,12},{12,0},{1,5},{5,9},{9,13},{13,1},{2,6},{6,10},{... | collective-permute-start | bytes 589832 | tf_op jit(solution)/shard_map/ppermute | solution.py:275
  18.2 2.2 %collective-permute-start.6 = (bf16[2,384,128]{2,1,0:T(8,128)(2,1)}, bf16[2,384,128]{2,1,0:T(8,128)(2,1)S(1)}, u32[]{:S(2)}, u32[]{:S(2)}) collective-permute-start(bf16[2,384,128]{2,1,0:T(8,128)(2,1)} %get-tuple-element.69), channel_id=1, source_target_pairs={{0,12},{4,0},{8,4},{12,8},{1,13},{5,1},{9,5},{13,9},{2,14},{6,2},{... | collective-permute-start | bytes 589832 | tf_op jit(solution)/shard_map/ppermute | solution.py:275
  20.5 0.0 copy-start.6
  20.5 1.6 %collective-permute-start.12 = (bf16[2,384,128]{2,1,0:T(8,128)(2,1)}, bf16[2,384,128]{2,1,0:T(8,128)(2,1)S(1)}, u32[]{:S(2)}, u32[]{:S(2)}) collective-permute-start(bf16[2,384,128]{2,1,0:T(8,128)(2,1)} %get-tuple-element.77.refs_0_), channel_id=1, source_target_pairs={{0,2},{2,0},{1,3},{3,1},{4,6},{6,4},{5,7},{7,5},{8,10},{10,8},{9,1... | collective-permute-start | bytes 589832 | tf_op jit(solution)/shard_map/ppermute | solution.py:275
  22.1 9.7 %shard_map.74 = (bf16[2,384,128]{2,1,0:T(8,128)(2,1)}, bf16[2,384,128]{2,1,0:T(8,128)(2,1)}, bf16[2,384,128]{2,1,0:T(8,128)(2,1)}, bf16[2,384,128]{2,1,0:T(8,128)(2,1)}) custom-call(s32[1024]{0:T(1024)} %bitcast.18, s32[512]{0:T(512)} %bitcast.10, bf16[256,12,8,2,128]{4,3,2,1,0:T(2,128)(2,1)} %bitcast.16, bf16[256,8,8,8,128]{4,3,2,1,0:T(8,128)(2,1)} %bitcast.14), custom_call_target="tpu_custom_call" | custom-call | flops 1024 | bytes 1024 | tf_op jit(solution)/shard_map/pallas_call | solution.py:135
  31.8 0.0 copy-start.1
  31.8 0.0 copy-start
  31.8 0.0 collective-permute-done.refs_1_
  31.8 1.1 %collective-permute-start.2 = (bf16[2,384,128]{2,1,0:T(8,128)(2,1)S(1)}, bf16[2,384,128]{2,1,0:T(8,128)(2,1)S(1)}, u32[]{:S(2)}, u32[]{:S(2)}) collective-permute-start(bf16[2,384,128]{2,1,0:T(8,128)(2,1)S(1)} %collective-permute-done.refs_1_), channel_id=1, source_target_pairs={{0,2},{2,0},{1,3},{3,1},{4,6},{6,4},{5,7},{7,5},{8,10},{10,8},{9,1... | collective-permute-start | bytes 589832 | tf_op jit(solution)/shard_map/ppermute | solution.py:275
  32.9 0.0 collective-permute-start.1
  32.9 0.0 collective-permute-done.3.refs_2_
  32.9 6.6 %collective-permute-start.4 = (bf16[2,384,128]{2,1,0:T(8,128)(2,1)}, bf16[2,384,128]{2,1,0:T(8,128)(2,1)S(1)}, u32[]{:S(2)}, u32[]{:S(2)}) collective-permute-start(bf16[2,384,128]{2,1,0:T(8,128)(2,1)} %get-tuple-element.62), channel_id=1, source_target_pairs={{0,4},{4,8},{8,12},{12,0},{1,5},{5,9},{9,13},{13,1},{2,6},{6,10},{... | collective-permute-start | bytes 589832 | tf_op jit(solution)/shard_map/ppermute | solution.py:275
  39.5 0.0 collective-permute-done.6.refs_3_
  39.5 1.5 %collective-permute-start.5 = (bf16[2,384,128]{2,1,0:T(8,128)(2,1)S(1)}, bf16[2,384,128]{2,1,0:T(8,128)(2,1)S(1)}, u32[]{:S(2)}, u32[]{:S(2)}) collective-permute-start(bf16[2,384,128]{2,1,0:T(8,128)(2,1)S(1)} %collective-permute-done.3.refs_2_), channel_id=1, source_target_pairs={{0,2},{2,0},{1,3},{3,1},{4,6},{6,4},{5,7},{7,5},{8,10},{10,8},{9,1... | collective-permute-start | bytes 589832 | tf_op jit(solution)/shard_map/ppermute | solution.py:275
  41.0 0.0 collective-permute-done.12.refs_5_
  41.0 0.0 collective-permute-start.7
  41.0 0.0 collective-permute-done.2.refs_6_
  41.1 0.6 collective-permute-start.8
  41.7 0.0 copy-done.2
  41.7 0.0 copy-done.3
  41.7 0.0 copy-done.4
  41.7 3.4 %shard_map.76.refs_6_ = bf16[768,2048]{1,0:T(8,128)(2,1)S(1)} custom-call(s32[6]{0:T(128)S(1)} %copy-done.4, s32[6]{0:T(128)S(1)} %copy-done.3, s32[512]{0:T(512)S(1)} %bitcast.11), custom_call_target="tpu_custom_call" | custom-call | flops 1024 | bytes 1024 | tf_op jit(solution)/shard_map/pallas_call | solution.py:196
  45.1 0.0 copy-done.5
  45.1 5.2 %shard_map.75.refs_10_ = bf16[1280,2048]{1,0:T(8,128)(2,1)S(1)} custom-call(s32[10]{0:T(128)S(1)} %copy-done.6, s32[10]{0:T(128)S(1)} %copy-done.5, s32[512]{0:T(512)S(1)} %bitcast.12), custom_call_target="tpu_custom_call" | custom-call | flops 1024 | bytes 1024 | tf_op jit(solution)/shard_map/pallas_call | solution.py:196
  50.3 0.0 collective-permute-done.1.refs_0_
  50.4 1.6 %collective-permute-start.13 = (bf16[2,384,128]{2,1,0:T(8,128)(2,1)S(1)}, bf16[2,384,128]{2,1,0:T(8,128)(2,1)S(1)}, u32[]{:S(2)}, u32[]{:S(2)}) collective-permute-start(bf16[2,384,128]{2,1,0:T(8,128)(2,1)S(1)} %copy-done.1), channel_id=1, source_target_pairs={{0,2},{2,0},{1,3},{3,1},{4,6},{6,4},{5,7},{7,5},{8,10},{10,8},{9,1... | collective-permute-start | bytes 589832 | tf_op jit(solution)/shard_map/ppermute | solution.py:275
  51.9 0.0 collective-permute-done.4.refs_1_
  51.9 0.0 collective-permute-done.5.refs_7_
  51.9 0.0 collective-permute-done.7.refs_2_
  51.9 0.0 collective-permute-done.8.refs_8_
  51.9 0.6 collective-permute-start.11
  52.5 1.5 %collective-permute-start.10 = (bf16[2,384,128]{2,1,0:T(8,128)(2,1)S(1)}, bf16[2,384,128]{2,1,0:T(8,128)(2,1)S(1)}, u32[]{:S(2)}, u32[]{:S(2)}) collective-permute-start(bf16[2,384,128]{2,1,0:T(8,128)(2,1)S(1)} %collective-permute-done.4.refs_1_), channel_id=1, source_target_pairs={{0,2},{2,0},{1,3},{3,1},{4,6},{6,4},{5,7},{7,5},{8,10},{10,8},{9,1... | collective-permute-start | bytes 589832 | tf_op jit(solution)/shard_map/ppermute | solution.py:275
  54.0 0.5 collective-permute-start.9
  54.6 3.7 %collective-permute-done.13.refs_9_ = bf16[2,384,128]{2,1,0:T(8,128)(2,1)S(1)} collective-permute-done((bf16[2,384,128]{2,1,0:T(8,128)(2,1)S(1)}, bf16[2,384,128]{2,1,0:T(8,128)(2,1)S(1)}, u32[]{:S(2)}, u32[]{:S(2)}) %collective-permute-start.13) | collective-permute-done | bytes 196640 | tf_op jit(solution)/shard_map/ppermute | solution.py:275
  58.3 0.0 copy-done
  58.3 5.9 %shard_map.77.refs_7_ = f32[768,2048]{1,0:T(8,128)S(1)} custom-call(bf16[2,384,128]{2,1,0:T(8,128)(2,1)S(1)} %copy-done, bf16[2,384,128]{2,1,0:T(8,128)(2,1)S(1)} %collective-permute-done.refs_1_, bf16[2,384,128]{2,1,0:T(8,128)(2,1)S(1)} %collective-permute-done.3.refs_2_, bf16[2,384,128]{2,1,0:T(8,128)(2,1)S(1)} %collective-permute-done.6.refs_3_, ...), custom_call_target="tpu_custom_call" | custom-call | flops 1024 | bytes 1024 | tf_op jit(solution)/shard_map/pallas_call | solution.py:261
  64.1 0.0 collective-permute-done.11.refs_5_
  64.2 2.5 %collective-permute-done.10.refs_4_ = bf16[2,384,128]{2,1,0:T(8,128)(2,1)S(1)} collective-permute-done((bf16[2,384,128]{2,1,0:T(8,128)(2,1)S(1)}, bf16[2,384,128]{2,1,0:T(8,128)(2,1)S(1)}, u32[]{:S(2)}, u32[]{:S(2)}) %collective-permute-start.10) | collective-permute-done | bytes 196640 | tf_op jit(solution)/shard_map/ppermute | solution.py:275
  66.7 2.3 %collective-permute-done.9.refs_3_ = bf16[2,384,128]{2,1,0:T(8,128)(2,1)S(1)} collective-permute-done((bf16[2,384,128]{2,1,0:T(8,128)(2,1)S(1)}, bf16[2,384,128]{2,1,0:T(8,128)(2,1)S(1)}, u32[]{:S(2)}, u32[]{:S(2)}) %collective-permute-start.9) | collective-permute-done | bytes 196640 | tf_op jit(solution)/shard_map/ppermute | solution.py:275
  68.9 4.9 %shard_map.78 = bf16[2,12,32,2048]{3,2,1,0:T(8,128)(2,1)} custom-call(bf16[2,384,128]{2,1,0:T(8,128)(2,1)S(1)} %collective-permute-done.1.refs_0_, bf16[2,384,128]{2,1,0:T(8,128)(2,1)S(1)} %collective-permute-done.4.refs_1_, bf16[2,384,128]{2,1,0:T(8,128)(2,1)S(1)} %collective-permute-done.7.refs_2_, ...), custom_call_target="tpu_custom_call" | custom-call | flops 1024 | bytes 1024 | tf_op jit(solution)/shard_map/pallas_call | solution.py:261
  (6 shorter events, 0.0 us)
Async XLA Ops:
  12.6 19.2 %collective-permute-start = (bf16[2,384,128]{2,1,0:T(8,128)(2,1)}, bf16[2,384,128]{2,1,0:T(8,128)(2,1)S(1)}, u32[]{:S(2)}, u32[]{:S(2)}) collective-permute-start(bf16[2,384,128]{2,1,0:T(8,128)(2,1)} %get-tuple-element.50), channel_id=1, source_target_pairs={{0,8},{4,12},{8,0},{12,4},{1,9},{5,13},{9,1},{13,5},{2,10},{6,14},... | collective-permute-start | bytes 589832 | tf_op jit(solution)/shard_map/ppermute | solution.py:275
  16.7 16.3 %collective-permute-start.3 = (bf16[2,384,128]{2,1,0:T(8,128)(2,1)}, bf16[2,384,128]{2,1,0:T(8,128)(2,1)S(1)}, u32[]{:S(2)}, u32[]{:S(2)}) collective-permute-start(bf16[2,384,128]{2,1,0:T(8,128)(2,1)} %get-tuple-element.61), channel_id=1, source_target_pairs={{0,4},{4,8},{8,12},{12,0},{1,5},{5,9},{9,13},{13,1},{2,6},{6,10},{... | collective-permute-start | bytes 589832 | tf_op jit(solution)/shard_map/ppermute | solution.py:275
  18.2 21.3 %collective-permute-start.6 = (bf16[2,384,128]{2,1,0:T(8,128)(2,1)}, bf16[2,384,128]{2,1,0:T(8,128)(2,1)S(1)}, u32[]{:S(2)}, u32[]{:S(2)}) collective-permute-start(bf16[2,384,128]{2,1,0:T(8,128)(2,1)} %get-tuple-element.69), channel_id=1, source_target_pairs={{0,12},{4,0},{8,4},{12,8},{1,13},{5,1},{9,5},{13,9},{2,14},{6,2},{... | collective-permute-start | bytes 589832 | tf_op jit(solution)/shard_map/ppermute | solution.py:275
  20.5 21.2 %copy-start.2 = (s32[4,128]{1,0:T(4,128)S(1)}, s32[4,128]{1,0:T(4,128)}, u32[]{:S(2)}) copy-start(s32[4,128]{1,0:T(4,128)} %select_reduce_fusion.1) | copy-start | bytes 6148
  20.5 21.2 %copy-start.3 = (s32[6]{0:T(128)S(1)}, s32[6]{0:T(128)}, u32[]{:S(2)}) copy-start(s32[6]{0:T(128)} %constant.13.clone.groups_ref) | copy-start | bytes 76
  20.5 21.2 %copy-start.4 = (s32[6]{0:T(128)S(1)}, s32[6]{0:T(128)}, u32[]{:S(2)}) copy-start(s32[6]{0:T(128)} %constant.12.clone.shifts_ref) | copy-start | bytes 76
  20.5 24.6 %copy-start.5 = (s32[10]{0:T(128)S(1)}, s32[10]{0:T(128)}, u32[]{:S(2)}) copy-start(s32[10]{0:T(128)} %constant.11.clone.groups_ref) | copy-start | bytes 124
  20.5 24.6 %copy-start.6 = (s32[10]{0:T(128)S(1)}, s32[10]{0:T(128)}, u32[]{:S(2)}) copy-start(s32[10]{0:T(128)} %constant.10.clone.shifts_ref) | copy-start | bytes 124
  20.5 20.5 %collective-permute-start.12 = (bf16[2,384,128]{2,1,0:T(8,128)(2,1)}, bf16[2,384,128]{2,1,0:T(8,128)(2,1)S(1)}, u32[]{:S(2)}, u32[]{:S(2)}) collective-permute-start(bf16[2,384,128]{2,1,0:T(8,128)(2,1)} %get-tuple-element.77.refs_0_), channel_id=1, source_target_pairs={{0,2},{2,0},{1,3},{3,1},{4,6},{6,4},{5,7},{7,5},{8,10},{10,8},{9,1... | collective-permute-start | bytes 589832 | tf_op jit(solution)/shard_map/ppermute | solution.py:275
  31.8 18.6 %copy-start.1 = (bf16[2,384,128]{2,1,0:T(8,128)(2,1)S(1)}, bf16[2,384,128]{2,1,0:T(8,128)(2,1)}, u32[]{:S(2)}) copy-start(bf16[2,384,128]{2,1,0:T(8,128)(2,1)} %get-tuple-element.81.refs_4_) | copy-start | bytes 589828
  31.8 26.5 %copy-start = (bf16[2,384,128]{2,1,0:T(8,128)(2,1)S(1)}, bf16[2,384,128]{2,1,0:T(8,128)(2,1)}, u32[]{:S(2)}) copy-start(bf16[2,384,128]{2,1,0:T(8,128)(2,1)} %get-tuple-element.77.refs_0_) | copy-start | bytes 589828
  31.8 9.2 %collective-permute-start.2 = (bf16[2,384,128]{2,1,0:T(8,128)(2,1)S(1)}, bf16[2,384,128]{2,1,0:T(8,128)(2,1)S(1)}, u32[]{:S(2)}, u32[]{:S(2)}) collective-permute-start(bf16[2,384,128]{2,1,0:T(8,128)(2,1)S(1)} %collective-permute-done.refs_1_), channel_id=1, source_target_pairs={{0,2},{2,0},{1,3},{3,1},{4,6},{6,4},{5,7},{7,5},{8,10},{10,8},{9,1... | collective-permute-start | bytes 589832 | tf_op jit(solution)/shard_map/ppermute | solution.py:275
  32.9 17.4 %collective-permute-start.1 = (bf16[2,384,128]{2,1,0:T(8,128)(2,1)}, bf16[2,384,128]{2,1,0:T(8,128)(2,1)S(1)}, u32[]{:S(2)}, u32[]{:S(2)}) collective-permute-start(bf16[2,384,128]{2,1,0:T(8,128)(2,1)} %get-tuple-element.51), channel_id=1, source_target_pairs={{0,8},{4,12},{8,0},{12,4},{1,9},{5,13},{9,1},{13,5},{2,10},{6,14},... | collective-permute-start | bytes 589832 | tf_op jit(solution)/shard_map/ppermute | solution.py:275
  32.9 19.0 %collective-permute-start.4 = (bf16[2,384,128]{2,1,0:T(8,128)(2,1)}, bf16[2,384,128]{2,1,0:T(8,128)(2,1)S(1)}, u32[]{:S(2)}, u32[]{:S(2)}) collective-permute-start(bf16[2,384,128]{2,1,0:T(8,128)(2,1)} %get-tuple-element.62), channel_id=1, source_target_pairs={{0,4},{4,8},{8,12},{12,0},{1,5},{5,9},{9,13},{13,1},{2,6},{6,10},{... | collective-permute-start | bytes 589832 | tf_op jit(solution)/shard_map/ppermute | solution.py:275
  39.5 12.4 %collective-permute-start.5 = (bf16[2,384,128]{2,1,0:T(8,128)(2,1)S(1)}, bf16[2,384,128]{2,1,0:T(8,128)(2,1)S(1)}, u32[]{:S(2)}, u32[]{:S(2)}) collective-permute-start(bf16[2,384,128]{2,1,0:T(8,128)(2,1)S(1)} %collective-permute-done.3.refs_2_), channel_id=1, source_target_pairs={{0,2},{2,0},{1,3},{3,1},{4,6},{6,4},{5,7},{7,5},{8,10},{10,8},{9,1... | collective-permute-start | bytes 589832 | tf_op jit(solution)/shard_map/ppermute | solution.py:275
  41.0 10.9 %collective-permute-start.7 = (bf16[2,384,128]{2,1,0:T(8,128)(2,1)}, bf16[2,384,128]{2,1,0:T(8,128)(2,1)S(1)}, u32[]{:S(2)}, u32[]{:S(2)}) collective-permute-start(bf16[2,384,128]{2,1,0:T(8,128)(2,1)} %get-tuple-element.70), channel_id=1, source_target_pairs={{0,12},{4,0},{8,4},{12,8},{1,13},{5,1},{9,5},{13,9},{2,14},{6,2},{... | collective-permute-start | bytes 589832 | tf_op jit(solution)/shard_map/ppermute | solution.py:275
  41.1 10.9 %collective-permute-start.8 = (bf16[2,384,128]{2,1,0:T(8,128)(2,1)S(1)}, bf16[2,384,128]{2,1,0:T(8,128)(2,1)S(1)}, u32[]{:S(2)}, u32[]{:S(2)}) collective-permute-start(bf16[2,384,128]{2,1,0:T(8,128)(2,1)S(1)} %collective-permute-done.6.refs_3_), channel_id=1, source_target_pairs={{0,2},{2,0},{1,3},{3,1},{4,6},{6,4},{5,7},{7,5},{8,10},{10,8},{9,1... | collective-permute-start | bytes 589832 | tf_op jit(solution)/shard_map/ppermute | solution.py:275
  50.4 7.9 %collective-permute-start.13 = (bf16[2,384,128]{2,1,0:T(8,128)(2,1)S(1)}, bf16[2,384,128]{2,1,0:T(8,128)(2,1)S(1)}, u32[]{:S(2)}, u32[]{:S(2)}) collective-permute-start(bf16[2,384,128]{2,1,0:T(8,128)(2,1)S(1)} %copy-done.1), channel_id=1, source_target_pairs={{0,2},{2,0},{1,3},{3,1},{4,6},{6,4},{5,7},{7,5},{8,10},{10,8},{9,1... | collective-permute-start | bytes 589832 | tf_op jit(solution)/shard_map/ppermute | solution.py:275
  51.9 12.2 %collective-permute-start.11 = (bf16[2,384,128]{2,1,0:T(8,128)(2,1)S(1)}, bf16[2,384,128]{2,1,0:T(8,128)(2,1)S(1)}, u32[]{:S(2)}, u32[]{:S(2)}) collective-permute-start(bf16[2,384,128]{2,1,0:T(8,128)(2,1)S(1)} %collective-permute-done.7.refs_2_), channel_id=1, source_target_pairs={{0,2},{2,0},{1,3},{3,1},{4,6},{6,4},{5,7},{7,5},{8,10},{10,8},{9,1... | collective-permute-start | bytes 589832 | tf_op jit(solution)/shard_map/ppermute | solution.py:275
  52.5 14.1 %collective-permute-start.10 = (bf16[2,384,128]{2,1,0:T(8,128)(2,1)S(1)}, bf16[2,384,128]{2,1,0:T(8,128)(2,1)S(1)}, u32[]{:S(2)}, u32[]{:S(2)}) collective-permute-start(bf16[2,384,128]{2,1,0:T(8,128)(2,1)S(1)} %collective-permute-done.4.refs_1_), channel_id=1, source_target_pairs={{0,2},{2,0},{1,3},{3,1},{4,6},{6,4},{5,7},{7,5},{8,10},{10,8},{9,1... | collective-permute-start | bytes 589832 | tf_op jit(solution)/shard_map/ppermute | solution.py:275
  54.0 14.9 %collective-permute-start.9 = (bf16[2,384,128]{2,1,0:T(8,128)(2,1)S(1)}, bf16[2,384,128]{2,1,0:T(8,128)(2,1)S(1)}, u32[]{:S(2)}, u32[]{:S(2)}) collective-permute-start(bf16[2,384,128]{2,1,0:T(8,128)(2,1)S(1)} %collective-permute-done.1.refs_0_), channel_id=1, source_target_pairs={{0,2},{2,0},{1,3},{3,1},{4,6},{6,4},{5,7},{7,5},{8,10},{10,8},{9,1... | collective-permute-start | bytes 589832 | tf_op jit(solution)/shard_map/ppermute | solution.py:275
